TPU v7x, 32 devices: a whole 2x2x4 slice. The times are simulated.
32 devices in a mesh: grp: 4 (over z), list: 8 (over y, x, core).
Axes of the slice: x: 2, y: 2, z: 4, core: 2. Of those that a mesh axis runs over, the one named last changes fastest.
Arguments:
- vectors: bfloat16 [3, 16384, 1024], P(None, ('grp', 'list')), may hold values from -6 to 6
- owner_route: int32 [3, 16384, 1], P(None, ('grp', 'list')), may hold values from 0 to 7; in each aligned block of 512 rows (0 to 511, 512 to 1023, ..., all dimensions but the last counted through in order) at most 128 rows name the same one
- list_slot: int32 [3, 16384], P(None, ('grp', 'list')), may hold values from 0 to 1023
- centroids: float32 [8192, 1024], P('list'), may hold values from -6 to 6
- counts: int32 [8192], P('list'), may hold values from 1 to 8
Outputs:
- residuals: bfloat16 [3, 16384, 1024], P(None, ('grp', 'list'))
- new_centroids: float32 [8192, 1024], P('list')
Inputs may be any that keep to these rules, and one draw needn't show every extreme that they name: `owner_route`: within the rows of one device for one step, at most 128 vectors name the same owner; some owner is named exactly 128 times.
All inputs are finite; a program needn't handle non-finite values.
Results may differ from a plain program's by a relative error of at most 0.0035.
Values may be sent and summed in bfloat16 or wider, within the bound.
A program may use at most 128 MiB of HBM per device.

v0:
```python
import jax
import jax.numpy as jnp
from jax import lax
from jax.sharding import PartitionSpec as P

STEPS = 3


def list_sums(slots, rows, list_dev):
    one_hot = (jnp.arange(list_dev, dtype=jnp.int32)[:, None] == slots[None, :]).astype(
        jnp.bfloat16
    )
    sums = jnp.dot(one_hot, rows, preferred_element_type=jnp.float32)
    return (sums, jnp.sum(one_hot, axis=1, dtype=jnp.float32))


def local(vectors, owner_route, list_slot, centroids, counts):
    owner_count = lax.axis_size("list")
    row_count = vectors.shape[1]
    width = vectors.shape[2]
    capacity = 2 * row_count // owner_count
    list_dev = centroids.shape[0]
    current = centroids
    weights = counts.astype(jnp.float32)
    outputs = []
    for step_index in range(STEPS):
        owner_ids = owner_route[step_index, :, 0]
        slot_ids = list_slot[step_index]
        owner_hits = (
            owner_ids[:, None] == jnp.arange(owner_count, dtype=jnp.int32)[None, :]
        ).astype(jnp.int32)
        rank_rows = jnp.sum((jnp.cumsum(owner_hits, axis=0) - owner_hits) * owner_hits, axis=1)
        dest_rows = owner_ids * capacity + rank_rows
        send_rows = (
            jnp.zeros((owner_count * capacity, width), jnp.bfloat16)
            .at[dest_rows]
            .set(vectors[step_index])
        )
        send_rows = send_rows.reshape(owner_count, capacity, width)
        send_slots = jnp.full((owner_count * capacity,), -1, jnp.int32).at[dest_rows].set(slot_ids)
        send_slots = send_slots.reshape(owner_count, capacity)
        table = current

        def route_fn(pieces, table=table):
            vec_rows, list_ids = pieces
            chosen = table[jnp.clip(list_ids, 0, list_dev - 1)]
            residual_rows = (vec_rows.astype(jnp.float32) - chosen).astype(jnp.bfloat16)
            back_rows = lax.all_to_all(
                residual_rows, "list", split_axis=0, concat_axis=0, tiled=True
            )
            return (back_rows, vec_rows, list_ids)

        back_rows, recv_rows, recv_slots = route_fn(
            (
                lax.all_to_all(send_rows, "list", split_axis=0, concat_axis=0, tiled=True),
                lax.all_to_all(send_slots, "list", split_axis=0, concat_axis=0, tiled=True),
            )
        )
        outputs.append(back_rows.reshape(owner_count * capacity, width)[dest_rows])
        flat_rows = recv_rows.reshape(-1, width)
        flat_slots = recv_slots.reshape(-1)
        sums, batch_count = list_sums(flat_slots, flat_rows, list_dev)
        total_sums, total_count = (
            lax.psum(sums.astype(jnp.bfloat16), "grp").astype(jnp.float32),
            lax.psum(batch_count.astype(jnp.bfloat16), "grp").astype(jnp.float32),
        )
        current = (weights[:, None] * current + total_sums) / (weights + total_count)[:, None]
        weights = weights + total_count
    return (jnp.stack(outputs, axis=0), current)


def solution(mesh):
    in_specs = (
        P(None, ("grp", "list"), None),
        P(None, ("grp", "list"), None),
        P(None, ("grp", "list")),
        P("list", None),
        P("list"),
    )
    out_specs = (P(None, ("grp", "list"), None), P("list", None))
    return jax.shard_map(local, mesh=mesh, in_specs=in_specs, out_specs=out_specs, check_vma=False)
```

profile of v0, /device:TPU:3, one launch (start us, length us, event | category | flops | bytes accessed | tf_op | source)
XLA Modules:
  0.0 459.6 jit_solution(8958284358738337007)
XLA Ops:
  13.9 3.0 scatter_custom_fusion.3
  16.9 4.6 all-to-all-start.4
  24.5 4.8 %all-to-all-start.7 = ((s32[8,1,128]{2,1,0:T(1,128)}), s32[8,1,128]{2,1,0:T(1,128)S(1)}, u32[]{:S(2)}, u32[]{:S(2)}) async-start(s32[8,1,128]{2,1,0:T(1,128)} %bitcast.49), calls=%async_computation.7 | async-start | bytes 8192 | tf_op jit(solution)/shard_map/all_to_all | solution.py:56
  32.3 4.9 %all-to-all-start.1 = ((s32[8,1,128]{2,1,0:T(1,128)}), s32[8,1,128]{2,1,0:T(1,128)S(1)}, u32[]{:S(2)}, u32[]{:S(2)}) async-start(s32[8,1,128]{2,1,0:T(1,128)} %bitcast.11), calls=%async_computation.1 | async-start | bytes 8192 | tf_op jit(solution)/shard_map/all_to_all | solution.py:56
  37.2 4.8 %scatter_custom_fusion.2 = bf16[1024,1024]{1,0:T(8,128)(2,1)} fusion(s32[512]{0:T(512)S(1)} %bitcast.137, bf16[3,512,1024]{2,1,0:T(8,128)(2,1)} %param.5, bf16[]{:T(256)} %constant.10.clone.1), kind=kCustom, calls=%fused_computation.39 | custom fusion | bytes 3146240 | tf_op jit(solution)/shard_map/scatter | solution.py:37
  42.0 4.2 all-to-all-start.3
  46.3 4.8 %scatter_custom_fusion.4 = bf16[1024,1024]{1,0:T(8,128)(2,1)} fusion(s32[512]{0:T(512)S(1)} %bitcast.140, bf16[3,512,1024]{2,1,0:T(8,128)(2,1)} %param.5, bf16[]{:T(256)} %constant.10.clone.1), kind=kCustom, calls=%fused_computation.37 | custom fusion | bytes 3146240 | tf_op jit(solution)/shard_map/scatter | solution.py:37
  51.1 20.2 %all-to-all-done.3 = bf16[8,128,1024]{2,1,0:T(8,128)(2,1)S(1)} async-done(((bf16[8,128,1024]{2,1,0:T(8,128)(2,1)}), bf16[8,128,1024]{2,1,0:T(8,128)(2,1)S(1)}, u32[]{:S(2)}, u32[]{:S(2)}) %all-to-all-start.3) | async-done | bytes 2097184 | tf_op jit(solution)/shard_map/all_to_all | solution.py:55
  71.3 5.8 %all-to-all-start.6 = ((bf16[8,128,1024]{2,1,0:T(8,128)(2,1)}), bf16[8,128,1024]{2,1,0:T(8,128)(2,1)}, u32[]{:S(2)}, u32[]{:S(2)}) async-start(bf16[8,128,1024]{2,1,0:T(8,128)(2,1)} %bitcast.45), calls=%async_computation.6 | async-start | bytes 4194304 | tf_op jit(solution)/shard_map/all_to_all | solution.py:55
  77.1 4.8 %scatter_custom_fusion = bf16[1024,1024]{1,0:T(8,128)(2,1)} fusion(s32[512]{0:T(512)S(1)} %bitcast.143, bf16[3,512,1024]{2,1,0:T(8,128)(2,1)} %param.5, bf16[]{:T(256)} %constant.10.clone.1), kind=kCustom, calls=%fused_computation.41 | custom fusion | bytes 3146240 | tf_op jit(solution)/shard_map/scatter | solution.py:37
  81.9 20.4 %all-to-all-done.6 = bf16[8,128,1024]{2,1,0:T(8,128)(2,1)} async-done(((bf16[8,128,1024]{2,1,0:T(8,128)(2,1)}), bf16[8,128,1024]{2,1,0:T(8,128)(2,1)}, u32[]{:S(2)}, u32[]{:S(2)}) %all-to-all-start.6) | async-done | bytes 2097184 | tf_op jit(solution)/shard_map/all_to_all | solution.py:55
  102.3 5.8 %all-to-all-start = ((bf16[8,128,1024]{2,1,0:T(8,128)(2,1)}), bf16[8,128,1024]{2,1,0:T(8,128)(2,1)}, u32[]{:S(2)}, u32[]{:S(2)}) async-start(bf16[8,128,1024]{2,1,0:T(8,128)(2,1)} %bitcast.8), calls=%async_computation | async-start | bytes 4194304 | tf_op jit(solution)/shard_map/all_to_all | solution.py:55
  108.1 3.7 fusion.13
  111.8 5.3 %fusion.14 = bf16[1024,1024]{1,0:T(8,128)(2,1)} fusion(bf16[1024,1024]{1,0:T(8,128)(2,1)} %bitcast.57, s32[1024]{0:T(1024)S(1)} %bitcast.128), kind=kOutput, calls=%fused_computation.36 | convolution fusion | flops 2149580800 | bytes 4198400 | tf_op jit(solution)/shard_map/dot_general | solution.py:13
  117.1 16.3 %all-to-all-done = bf16[8,128,1024]{2,1,0:T(8,128)(2,1)} async-done(((bf16[8,128,1024]{2,1,0:T(8,128)(2,1)}), bf16[8,128,1024]{2,1,0:T(8,128)(2,1)}, u32[]{:S(2)}, u32[]{:S(2)}) %all-to-all-start) | async-done | bytes 2097184 | tf_op jit(solution)/shard_map/all_to_all | solution.py:55
  133.3 5.2 %fusion.12 = bf16[1024,1024]{1,0:T(8,128)(2,1)} fusion(bf16[1024,1024]{1,0:T(8,128)(2,1)} %bitcast.28, s32[1024]{0:T(1024)S(1)} %bitcast.131), kind=kOutput, calls=%fused_computation.34 | convolution fusion | flops 2149580800 | bytes 4198400 | tf_op jit(solution)/shard_map/dot_general | solution.py:13
  139.2 8.5 %gather_fusion = f32[1024,1024]{1,0:T(8,128)} fusion(f32[1024,1024]{1,0:T(8,128)} %param.8, s32[1024]{0:T(1024)S(1)} %fusion.37), kind=kCustom, calls=%fused_computation | custom fusion | bytes 8392704 | tf_op jit(solution)/shard_map/gather | solution.py:46
  149.3 10.8 %all-reduce = (bf16[1024]{0:T(1024)(128)(2,1)S(1)}, bf16[1024]{0:T(1024)(128)(2,1)S(1)}, bf16[1024]{0:T(1024)(128)(2,1)S(1)}) all-reduce(bf16[1024]{0:T(1024)(128)(2,1)S(1)} %fusion.6, bf16[1024]{0:T(1024)(128)(2,1)S(1)} %fusion.7, bf16[1024]{0:T(1024)(128)(2,1)S(1)} %fusion.8), channel_id=1, replica_groups=mesh['grp'=4,'list'=8] {'grp'}, use_global_device_ids=true, to_apply=%region_11.12 | all-reduce | flops 3072 | bytes 12288 | tf_op jit(solution)/shard_map/psum | solution.py:65
  160.1 5.0 %subtract_convert_fusion.2 = bf16[8,128,1024]{2,1,0:T(8,128)(2,1)} fusion(f32[8,128,1024]{2,1,0:T(8,128)} %bitcast.112, bf16[8,128,1024]{2,1,0:T(8,128)(2,1)} %all-to-all-done), kind=kLoop, calls=%fused_computation.26 | loop fusion | flops 3145728 | bytes 8388608 | tf_op jit(solution)/shard_map/convert_element_type | solution.py:47
  165.1 7.1 %all-to-all-start.2 = ((bf16[8,128,1024]{2,1,0:T(8,128)(2,1)}), bf16[8,128,1024]{2,1,0:T(8,128)(2,1)S(1)}, u32[]{:S(2)}, u32[]{:S(2)}) async-start(bf16[8,128,1024]{2,1,0:T(8,128)(2,1)} %subtract_convert_fusion.2), calls=%async_computation.2 | async-start | bytes 4194304 | tf_op jit(solution)/shard_map/all_to_all | solution.py:48
  172.3 190.6 %all-reduce.4.cloned.1.call-done = (bf16[1024,1024]{1,0:T(8,128)(2,1)}, bf16[1024,1024]{1,0:T(8,128)(2,1)}, bf16[1024,1024]{1,0:T(8,128)(2,1)}) async-done(((bf16[1024,1024]{1,0:T(8,128)(2,1)}, bf16[1024,1024]{1,0:T(8,128)(2,1)}, bf16[1024,1024]{1,0:T(8,128)(2,1)}), (bf16[1024,1024]{1,0:T(8,128)(2,1)}, bf16[1024,1024]{1,0:T(8,128)(2,1)}, bf16[1024,1024]{1,0:T(8,128)(2,1)})) %all-reduce.4.cloned.1.call-update) | async-done | bytes 6291472 | tf_op jit(solution)/shard_map/psum | solution.py:64
  362.9 8.4 %add_divide_fusion = (f32[1024,1024]{1,0:T(8,128)}, f32[1024,1024]{1,0:T(8,128)}, f32[1024,1024]{1,0:T(8,128)}) fusion(bf16[1024,1024]{1,0:T(8,128)(2,1)} %get-tuple-element.7, f32[1024]{0:T(1024)S(1)} %get-tuple-element.11, f32[1024]{0:T(1024)S(1)} %get-tuple-element.12, bf16[1024,1024]{1,0:T(8,128)(2,1)} %get-tuple-element.5, ...), kind=kLoop, calls=%fused_computation.12 | loop fusion | flops 12582912 | bytes 23085056 | tf_op jit(solution)/shard_map/div | solution.py:67
  371.3 8.6 %gather_fusion.4 = f32[1024,1024]{1,0:T(8,128)} fusion(f32[1024,1024]{1,0:T(8,128)} %get-tuple-element.9, s32[1024]{0:T(1024)S(1)} %fusion.41), kind=kCustom, calls=%fused_computation.4 | custom fusion | bytes 8392704 | tf_op jit(solution)/shard_map/gather | solution.py:46
  379.9 5.0 %subtract_convert_fusion = bf16[8,128,1024]{2,1,0:T(8,128)(2,1)} fusion(f32[8,128,1024]{2,1,0:T(8,128)} %bitcast.113, bf16[8,128,1024]{2,1,0:T(8,128)(2,1)} %all-to-all-done.6), kind=kLoop, calls=%fused_computation.16 | loop fusion | flops 3145728 | bytes 8388608 | tf_op jit(solution)/shard_map/convert_element_type | solution.py:47
  384.9 5.1 %all-to-all-start.8 = ((bf16[8,128,1024]{2,1,0:T(8,128)(2,1)}), bf16[8,128,1024]{2,1,0:T(8,128)(2,1)}, u32[]{:S(2)}, u32[]{:S(2)}) async-start(bf16[8,128,1024]{2,1,0:T(8,128)(2,1)} %subtract_convert_fusion), calls=%async_computation.8 | async-start | bytes 4194304 | tf_op jit(solution)/shard_map/all_to_all | solution.py:48
  390.0 8.6 %gather_fusion.2 = f32[1024,1024]{1,0:T(8,128)} fusion(f32[1024,1024]{1,0:T(8,128)} %get-tuple-element.10, s32[1024]{0:T(1024)S(1)} %fusion.39), kind=kCustom, calls=%fused_computation.2 | custom fusion | bytes 8392704 | tf_op jit(solution)/shard_map/gather | solution.py:46
  398.6 4.9 %subtract_convert_fusion.1 = bf16[8,128,1024]{2,1,0:T(8,128)(2,1)} fusion(f32[8,128,1024]{2,1,0:T(8,128)} %bitcast.114, bf16[8,128,1024]{2,1,0:T(8,128)(2,1)} %copy-done), kind=kLoop, calls=%fused_computation.21 | loop fusion | flops 3145728 | bytes 8388608 | tf_op jit(solution)/shard_map/convert_element_type | solution.py:47
  403.5 11.6 %all-to-all-done.8 = bf16[8,128,1024]{2,1,0:T(8,128)(2,1)} async-done(((bf16[8,128,1024]{2,1,0:T(8,128)(2,1)}), bf16[8,128,1024]{2,1,0:T(8,128)(2,1)}, u32[]{:S(2)}, u32[]{:S(2)}) %all-to-all-start.8) | async-done | bytes 2097184 | tf_op jit(solution)/shard_map/all_to_all | solution.py:48
  415.1 5.8 %all-to-all-start.5 = ((bf16[8,128,1024]{2,1,0:T(8,128)(2,1)}), bf16[8,128,1024]{2,1,0:T(8,128)(2,1)}, u32[]{:S(2)}, u32[]{:S(2)}) async-start(bf16[8,128,1024]{2,1,0:T(8,128)(2,1)} %subtract_convert_fusion.1), calls=%async_computation.5 | async-start | bytes 4194304 | tf_op jit(solution)/shard_map/all_to_all | solution.py:48
  423.1 4.6 gather_fusion.5
  427.7 18.5 %all-to-all-done.5 = bf16[8,128,1024]{2,1,0:T(8,128)(2,1)} async-done(((bf16[8,128,1024]{2,1,0:T(8,128)(2,1)}), bf16[8,128,1024]{2,1,0:T(8,128)(2,1)}, u32[]{:S(2)}, u32[]{:S(2)}) %all-to-all-start.5) | async-done | bytes 2097184 | tf_op jit(solution)/shard_map/all_to_all | solution.py:48
  446.1 4.6 gather_fusion.3
  (49 shorter events, 19.1 us)
Async XLA Ops:
  16.9 7.6 %all-to-all-start.4 = ((s32[8,1,128]{2,1,0:T(1,128)}), s32[8,1,128]{2,1,0:T(1,128)S(1)}, u32[]{:S(2)}, u32[]{:S(2)}) async-start(s32[8,1,128]{2,1,0:T(1,128)} %bitcast.30), calls=%async_computation.4 | async-start | bytes 8192 | tf_op jit(solution)/shard_map/all_to_all | solution.py:56
  24.5 7.8 %all-to-all-start.7 = ((s32[8,1,128]{2,1,0:T(1,128)}), s32[8,1,128]{2,1,0:T(1,128)S(1)}, u32[]{:S(2)}, u32[]{:S(2)}) async-start(s32[8,1,128]{2,1,0:T(1,128)} %bitcast.49), calls=%async_computation.7 | async-start | bytes 8192 | tf_op jit(solution)/shard_map/all_to_all | solution.py:56
  32.3 9.7 %all-to-all-start.1 = ((s32[8,1,128]{2,1,0:T(1,128)}), s32[8,1,128]{2,1,0:T(1,128)S(1)}, u32[]{:S(2)}, u32[]{:S(2)}) async-start(s32[8,1,128]{2,1,0:T(1,128)} %bitcast.11), calls=%async_computation.1 | async-start | bytes 8192 | tf_op jit(solution)/shard_map/all_to_all | solution.py:56
  42.0 29.3 %all-to-all-start.3 = ((bf16[8,128,1024]{2,1,0:T(8,128)(2,1)}), bf16[8,128,1024]{2,1,0:T(8,128)(2,1)S(1)}, u32[]{:S(2)}, u32[]{:S(2)}) async-start(bf16[8,128,1024]{2,1,0:T(8,128)(2,1)} %bitcast.26), calls=%async_computation.3 | async-start | bytes 4194304 | tf_op jit(solution)/shard_map/all_to_all | solution.py:55
  71.3 36.8 %copy-start = (bf16[8,128,1024]{2,1,0:T(8,128)(2,1)}, bf16[8,128,1024]{2,1,0:T(8,128)(2,1)S(1)}, u32[]{:S(2)}) copy-start(bf16[8,128,1024]{2,1,0:T(8,128)(2,1)S(1)} %all-to-all-done.3) | copy-start | bytes 6291460
  71.3 31.0 %all-to-all-start.6 = ((bf16[8,128,1024]{2,1,0:T(8,128)(2,1)}), bf16[8,128,1024]{2,1,0:T(8,128)(2,1)}, u32[]{:S(2)}, u32[]{:S(2)}) async-start(bf16[8,128,1024]{2,1,0:T(8,128)(2,1)} %bitcast.45), calls=%async_computation.6 | async-start | bytes 4194304 | tf_op jit(solution)/shard_map/all_to_all | solution.py:55
  102.3 31.0 %all-to-all-start = ((bf16[8,128,1024]{2,1,0:T(8,128)(2,1)}), bf16[8,128,1024]{2,1,0:T(8,128)(2,1)}, u32[]{:S(2)}, u32[]{:S(2)}) async-start(bf16[8,128,1024]{2,1,0:T(8,128)(2,1)} %bitcast.8), calls=%async_computation | async-start | bytes 4194304 | tf_op jit(solution)/shard_map/all_to_all | solution.py:55
  108.1 254.8 %all-reduce.4.cloned.1.call-start = ((), (), s32[]{:S(2)}) async-start(), calls=%async_computation.9 | async-start | bytes 12582912 | tf_op jit(solution)/shard_map/psum | solution.py:64
  138.5 0.7 copy-start.1
  165.1 219.7 %all-to-all-start.2 = ((bf16[8,128,1024]{2,1,0:T(8,128)(2,1)}), bf16[8,128,1024]{2,1,0:T(8,128)(2,1)S(1)}, u32[]{:S(2)}, u32[]{:S(2)}) async-start(bf16[8,128,1024]{2,1,0:T(8,128)(2,1)} %subtract_convert_fusion.2), calls=%async_computation.2 | async-start | bytes 4194304 | tf_op jit(solution)/shard_map/all_to_all | solution.py:48
  384.9 30.3 %all-to-all-start.8 = ((bf16[8,128,1024]{2,1,0:T(8,128)(2,1)}), bf16[8,128,1024]{2,1,0:T(8,128)(2,1)}, u32[]{:S(2)}, u32[]{:S(2)}) async-start(bf16[8,128,1024]{2,1,0:T(8,128)(2,1)} %subtract_convert_fusion), calls=%async_computation.8 | async-start | bytes 4194304 | tf_op jit(solution)/shard_map/all_to_all | solution.py:48
  415.1 31.0 %all-to-all-start.5 = ((bf16[8,128,1024]{2,1,0:T(8,128)(2,1)}), bf16[8,128,1024]{2,1,0:T(8,128)(2,1)}, u32[]{:S(2)}, u32[]{:S(2)}) async-start(bf16[8,128,1024]{2,1,0:T(8,128)(2,1)} %subtract_convert_fusion.1), calls=%async_computation.5 | async-start | bytes 4194304 | tf_op jit(solution)/shard_map/all_to_all | solution.py:48
Sparse Core Ops, SparseCore 0:
  138.7 224.1 all-reduce.3
where the time goes:
time: 463 us; the launch traced here: 460 us
  waiting for transfers between devices  278 us (60%)
  local copies, waits for them, and re-layouts  63.3 us (14%)
  starting transfers between devices  48.2 us (10%)
  other arithmetic  31.4 us (7%)
  matrix products  14.1 us (3%)
  between operations  14.1 us (3%)
  blocking collectives  10.8 us (2%)
    psum x1, waiting for transfers between devices, local(): lax.psum(sums.astype(jnp.bfloat16), 'grp').astype(jnp.float32)  191 us
    all_to_all x3, waiting for transfers between devices, local(): lax.all_to_all(send_rows, 'list', split_axis=0, concat_axis=0, tiled=True)  56.9 us
    all_to_all x3, waiting for transfers between devices, route_fn(): lax.all_to_all(residual_rows, 'list', split_axis=0, concat_axis=0, tiled=...  30.1 us
    gather x3, local copies, waits for them, and re-layouts, route_fn(): chosen = table[jnp.clip(list_ids, 0, list_dev - 1)]  25.8 us
    all_to_all x3, starting transfers between devices, route_fn(): lax.all_to_all(residual_rows, 'list', split_axis=0, concat_axis=0, tiled=...  18.1 us
    all_to_all x3, starting transfers between devices, local(): lax.all_to_all(send_rows, 'list', split_axis=0, concat_axis=0, tiled=True)  15.9 us
    convert_element_type x3, other arithmetic, route_fn(): residual_rows = (vec_rows.astype(jnp.float32) - chosen).astype(jnp.bfloat16)  14.9 us
    scatter x3, local copies, waits for them, and re-layouts, local(): send_rows = jnp.zeros((owner_count * capacity, width), jnp.bfloat16).at[d...  14.4 us
  transfers between devices with their start and end apart: 10, of which 6 were waited for; matrix products, arithmetic and copies ran while one was open for 19% of the time, Pallas kernels for 0%

commit v1 on v0

v1 whole, which is shorter than its diff:
```python
import functools

import jax
import jax.numpy as jnp
from jax import lax
from jax.experimental import pallas as pl
from jax.experimental.pallas import tpu as pltpu
from jax.sharding import PartitionSpec as P

MESH = pl.DeviceIdType.MESH
BF16 = jnp.bfloat16
F32 = jnp.float32
I32 = jnp.int32


def one_hot(mask):
    return jnp.where(mask, 1.0, 0.0).astype(BF16)


def dot(a, b):
    return jnp.dot(a, b, preferred_element_type=F32)


def loop(count, body):
    def step(i, carry):
        body(i)
        return carry

    lax.fori_loop(0, count, step, 0)


def rows_at(start, size):
    return pl.ds(pl.multiple_of(start, size), size)


def kernel(
    dims,
    vec_hbm, owner_ref, slot_ref, cent_hbm, counts_ref,
    out_hbm, new_hbm,
    vec, send, recv, back, part, from_left, from_right, num, high, low,
    send_slots, recv_slots, slot_row, slot_col, dest_row, dest_col, count_col, count_msg, weight_col,
    load_sem, out_sem, slot_send, slot_recv, disp_send, disp_recv, ret_send, ret_recv,
    right_send, left_send, left_recv, right_recv, cnt_send, cnt_recv,
):
    steps, rows, width, owners, groups, lists, cap = dims
    places = owners * cap
    quarter = lists // groups
    pack = 128 // cap
    me = lax.axis_index("list")
    z = lax.axis_index("grp")

    loads = [pltpu.make_async_copy(vec_hbm.at[s], vec.at[s], load_sem.at[s]) for s in range(steps)]
    loads.append(pltpu.make_async_copy(cent_hbm, num, load_sem.at[steps]))
    for load in loads:
        load.start()

    barrier = pltpu.get_barrier_semaphore()

    def greet_owner(i):
        pl.semaphore_signal(barrier, inc=1, device_id={"list": lax.rem(me + i + 1, owners)}, device_id_type=MESH)

    def greet_group(i):
        pl.semaphore_signal(barrier, inc=1, device_id={"grp": lax.rem(z + i + 1, groups)}, device_id_type=MESH)

    loop(owners - 1, greet_owner)
    loop(groups - 1, greet_group)

    owner_iota = lax.broadcasted_iota(I32, (owners, rows), 0)
    before = one_hot(
        lax.broadcasted_iota(I32, (rows, rows), 0) < lax.broadcasted_iota(I32, (rows, rows), 1)
    )
    hits, ranks, dests = [], [], []
    for s in range(steps):
        hit = jnp.where(owner_iota == owner_ref[s : s + 1, :], 1.0, 0.0)
        rank = hit * dot(hit.astype(BF16), before)
        hits.append(hit)
        ranks.append(jnp.sum(rank, axis=0, keepdims=True))
        dests.append(jnp.sum(rank + hit * (owner_iota * cap).astype(F32), axis=0, keepdims=True))
        dest_row[s : s + 1, :] = dests[s].astype(I32)
    table = jnp.concatenate(dests + ranks + [jnp.zeros((128 - 2 * steps, rows), F32)], axis=0)
    dest_col[...] = jnp.transpose(table).astype(I32)

    send_slots[...] = jnp.zeros_like(send_slots)
    lane = lax.broadcasted_iota(I32, (rows, 128), 1)
    for s in range(steps):
        value = slot_ref[s : s + 1, :] + 1
        upper = (value // 32).astype(F32)
        lower = (value % 32).astype(F32)
        spot = one_hot(lane == dest_col[:, steps + s : steps + s + 1] + lax.rem(me, pack) * cap)
        line = 32.0 * dot((hits[s] * upper).astype(BF16), spot) + dot((hits[s] * lower).astype(BF16), spot)
        for p in range(owners):
            send_slots[p, s : s + 1, :] = line[p : p + 1, :]
    recv_slots[me] = send_slots[me]

    pl.semaphore_wait(barrier, owners - 1 + groups - 1)

    def send_slot(i):
        p = lax.rem(me + i + 1, owners)
        pltpu.make_async_remote_copy(
            src_ref=send_slots.at[p], dst_ref=recv_slots.at[me], send_sem=slot_send, recv_sem=slot_recv,
            device_id={"list": p}, device_id_type=MESH,
        ).start()

    loop(owners - 1, send_slot)

    tile = min(256, places)

    def pack_rows(s):
        loads[s].wait()

        def body(i):
            at = rows_at(i * tile, tile)
            place = lax.broadcasted_iota(I32, (tile, rows), 0) + i * tile
            send[s, at, :] = dot(one_hot(place == dest_row[s : s + 1, :]), vec[s]).astype(BF16)

        loop(places // tile, body)
        mine = rows_at(me * cap, cap)
        recv[s, mine, :] = send[s, mine, :]

    def exchange(src, dst, s, send_sem, recv_sem):
        def body(i):
            p = lax.rem(me + i + 1, owners)
            pltpu.make_async_remote_copy(
                src_ref=src.at[s, rows_at(p * cap, cap)], dst_ref=dst.at[s, rows_at(me * cap, cap)],
                send_sem=send_sem.at[s], recv_sem=recv_sem.at[s],
                device_id={"list": p}, device_id_type=MESH,
            ).start()

        loop(owners - 1, body)

    def drain(ref, s, sem):
        others = ref.at[s, pl.ds(0, (owners - 1) * cap)]
        pltpu.make_async_copy(others, others, sem.at[s]).wait()

    def split_table():
        def body(i):
            at = rows_at(i * quarter, quarter)
            value = num[at, :]
            top = value.astype(BF16)
            high[at, :] = top
            low[at, :] = (value - top.astype(F32)).astype(BF16)

        loop(groups, body)

    def get_slots():
        others = recv_slots.at[pl.ds(0, owners - 1)]
        pltpu.make_async_copy(others, others, slot_recv).wait()
        chunks = []
        for c in range(owners // pack):
            chunk = recv_slots[c * pack]
            for i in range(1, pack):
                chunk = chunk + recv_slots[c * pack + i]
            chunks.append(chunk)
        line = jnp.concatenate(chunks, axis=1) - 1.0
        slot_row[...] = line.astype(I32)
        tall = jnp.concatenate([line, jnp.zeros((120, places), F32)], axis=0)
        slot_col[...] = jnp.transpose(tall).astype(I32)
        count_col[...] = jnp.zeros_like(count_col)

    def list_sums(s):
        def body(i):
            at = rows_at(i * quarter, quarter)
            name = lax.broadcasted_iota(I32, (quarter, places), 0) + i * quarter
            mask = jnp.where(name == slot_row[s : s + 1, :], 1.0, 0.0)
            part[s, i] = dot(mask.astype(BF16), recv[s]).astype(BF16)
            column = lax.broadcasted_iota(I32, (quarter, 128), 1)
            count_col[at, :] = jnp.where(column == s, jnp.sum(mask, axis=1, keepdims=True), count_col[at, :])

        loop(groups, body)

    def residual(s):
        def body(i):
            at = rows_at(i * tile, tile)
            pick = one_hot(lax.broadcasted_iota(I32, (tile, lists), 1) == slot_col[at, s : s + 1])
            chosen = dot(pick, high[...]) + dot(pick, low[...])
            recv[s, at, :] = (recv[s, at, :].astype(F32) - chosen).astype(BF16)

        loop(places // tile, body)
        mine = rows_at(me * cap, cap)
        back[s, mine, :] = recv[s, mine, :]
        exchange(recv, back, s, ret_send, ret_recv)

    out_tile = min(256, rows)

    def unpack_rows(s):
        drain(back, s, ret_recv)

        def body(i):
            at = rows_at(i * out_tile, out_tile)
            pick = one_hot(lax.broadcasted_iota(I32, (out_tile, places), 1) == dest_col[at, s : s + 1])
            vec[s, at, :] = dot(pick, back[s]).astype(BF16)

        loop(rows // out_tile, body)
        pltpu.make_async_copy(vec.at[s], out_hbm.at[s], out_sem.at[s]).start()

    def send_counts():
        count_msg[z] = jnp.transpose(count_col[...])[0:8, :]

        def body(i):
            g = lax.rem(z + i + 1, groups)
            pltpu.make_async_remote_copy(
                src_ref=count_msg.at[z], dst_ref=count_msg.at[z], send_sem=cnt_send, recv_sem=cnt_recv,
                device_id={"grp": g}, device_id_type=MESH,
            ).start()

        loop(groups - 1, body)

    def get_counts():
        others = count_msg.at[pl.ds(0, groups - 1)]
        pltpu.make_async_copy(others, others, cnt_recv).wait()
        total = count_msg[0]
        for g in range(1, groups):
            total = total + count_msg[g]
        lines = [counts_ref[...].astype(F32)]
        for s in range(steps):
            lines.append(lines[-1] + total[s : s + 1, :])
        lines.append(jnp.ones((128 - len(lines), lists), F32))
        weight_col[...] = jnp.transpose(jnp.concatenate(lines, axis=0))

    def update(s, last):
        def body(q):
            at = rows_at(q * quarter, quarter)
            after = weight_col[at, s + 1 : s + 2]

            def add(ref):
                value = num[at, :]
                if s == 0:
                    value = value * weight_col[at, 0:1]
                value = value + ref[s, q].astype(F32)
                mean = value * (1.0 / after)
                if last:
                    num[at, :] = mean
                else:
                    num[at, :] = value
                    top = mean.astype(BF16)
                    high[at, :] = top
                    low[at, :] = (mean - top.astype(F32)).astype(BF16)

            @pl.when(q < z)
            def _():
                add(from_left)

            @pl.when(q == z)
            def _():
                add(part)

            @pl.when(q > z)
            def _():
                add(from_right)

        loop(groups, body)

    def to_right(src, s, q):
        return pltpu.make_async_remote_copy(
            src_ref=src.at[s, q], dst_ref=from_left.at[s, q], send_sem=right_send, recv_sem=left_recv.at[s, q],
            device_id={"grp": lax.rem(z + 1, groups)}, device_id_type=MESH,
        )

    def to_left(src, s, q):
        return pltpu.make_async_remote_copy(
            src_ref=src.at[s, q], dst_ref=from_right.at[s, q], send_sem=left_send, recv_sem=right_recv.at[s, q],
            device_id={"grp": lax.rem(z + groups - 1, groups)}, device_id_type=MESH,
        )

    def wait_left(s, q):
        pltpu.make_async_copy(from_left.at[s, q], from_left.at[s, q], left_recv.at[s, q]).wait()

    def wait_right(s, q):
        pltpu.make_async_copy(from_right.at[s, q], from_right.at[s, q], right_recv.at[s, q]).wait()

    def add_into(ref, s, q):
        ref[s, q] = (ref[s, q].astype(F32) + part[s, q].astype(F32)).astype(BF16)

    def reduce_hop(s, t):
        @pl.when(z == t)
        def _():
            for q in range(groups - 1, t, -1):
                if t > 0:
                    wait_left(s, q)
                    add_into(from_left, s, q)
                    to_right(from_left, s, q).start()
                else:
                    to_right(part, s, q).start()

        @pl.when(z == groups - 1 - t)
        def _():
            for q in range(groups - 1 - t):
                if t > 0:
                    wait_right(s, q)
                    add_into(from_right, s, q)
                    to_left(from_right, s, q).start()
                else:
                    to_left(part, s, q).start()

    def total(s):
        @pl.when(z > 0)
        def _():
            wait_left(s, z)

        @pl.when(z < groups - 1)
        def _():
            wait_right(s, z)

        @pl.when(z == 0)
        def _():
            add_into_part(s, (from_right,))

        @pl.when(z == groups - 1)
        def _():
            add_into_part(s, (from_left,))

        @pl.when((z > 0) & (z < groups - 1))
        def _():
            add_into_part(s, (from_left, from_right))

    def add_into_part(s, refs):
        value = part[s, z].astype(F32)
        for ref in refs:
            value = value + ref[s, z].astype(F32)
        part[s, z] = value.astype(BF16)

    def share_own(s):
        @pl.when(z < groups - 1)
        def _():
            to_right(part, s, z).start()

        @pl.when(z > 0)
        def _():
            to_left(part, s, z).start()

    def share_hop(s, t):
        @pl.when(z - t >= 0)
        def _():
            q = z - t
            wait_left(s, q)

            @pl.when(z < groups - 1)
            def _():
                to_right(from_left, s, q).start()

        @pl.when(z + t < groups)
        def _():
            q = z + t
            wait_right(s, q)

            @pl.when(z > 0)
            def _():
                to_left(from_right, s, q).start()

    pack_rows(0)
    exchange(send, recv, 0, disp_send, disp_recv)
    pack_rows(1)
    pack_rows(2)
    get_slots()
    loads[steps].wait()
    split_table()
    drain(recv, 0, disp_recv)
    exchange(send, recv, 1, disp_send, disp_recv)
    list_sums(0)

    def hook(k, t):
        if (k, t) == (0, 0):
            residual(0)
        elif (k, t) == (0, 1):
            drain(recv, 1, disp_recv)
            exchange(send, recv, 2, disp_send, disp_recv)
            list_sums(1)
        elif (k, t) == (1, 0):
            drain(recv, 2, disp_recv)
            list_sums(2)
            send_counts()
        elif (k, t) == (1, 1):
            unpack_rows(0)
            get_counts()
        elif (k, t) == (2, 0):
            update(0, False)
            residual(1)
        elif (k, t) == (3, 0):
            update(1, False)
            residual(2)
        elif (k, t) == (3, 1):
            unpack_rows(1)

    for k in range(steps + 1):
        if k > 0:
            share_own(k - 1)
        for t in range(groups - 1):
            if k < steps:
                reduce_hop(k, t)
            hook(k, t)
            if k > 0:
                share_hop(k - 1, t + 1)
        if k < steps:
            total(k)

    update(steps - 1, True)
    store = pltpu.make_async_copy(num, new_hbm, out_sem.at[steps])
    store.start()
    unpack_rows(2)

    others = send_slots.at[pl.ds(0, owners - 1)]
    pltpu.make_async_copy(others, others, slot_send).wait()
    others = count_msg.at[pl.ds(0, groups - 1)]
    pltpu.make_async_copy(others, others, cnt_send).wait()
    for s in range(steps):
        drain(send, s, disp_send)
        drain(recv, s, ret_send)
        pltpu.make_async_copy(vec.at[s], out_hbm.at[s], out_sem.at[s]).wait()

    @pl.when(z < groups - 1)
    def _():
        pltpu.make_async_copy(from_left, from_left, right_send).wait()

    @pl.when(z > 0)
    def _():
        pltpu.make_async_copy(from_right, from_right, left_send).wait()

    store.wait()


def local(vectors, owner_route, list_slot, centroids, counts):
    steps, rows, width = vectors.shape
    owners = lax.axis_size("list")
    groups = lax.axis_size("grp")
    lists = centroids.shape[0]
    cap = 2 * rows // owners
    places = owners * cap
    quarter = lists // groups
    dims = (steps, rows, width, owners, groups, lists, cap)
    vmem = pl.BlockSpec(memory_space=pltpu.VMEM)
    hbm = pl.BlockSpec(memory_space=pl.ANY)
    dma = pltpu.SemaphoreType.DMA
    return pl.pallas_call(
        functools.partial(kernel, dims),
        out_shape=(
            jax.ShapeDtypeStruct((steps, rows, width), BF16),
            jax.ShapeDtypeStruct((lists, width), F32),
        ),
        in_specs=[hbm, vmem, vmem, hbm, vmem],
        out_specs=(hbm, hbm),
        scratch_shapes=[
            pltpu.VMEM((steps, rows, width), BF16),
            pltpu.VMEM((steps, places, width), BF16),
            pltpu.VMEM((steps, places, width), BF16),
            pltpu.VMEM((steps, places, width), BF16),
            pltpu.VMEM((steps, groups, quarter, width), BF16),
            pltpu.VMEM((steps, groups, quarter, width), BF16),
            pltpu.VMEM((steps, groups, quarter, width), BF16),
            pltpu.VMEM((lists, width), F32),
            pltpu.VMEM((lists, width), BF16),
            pltpu.VMEM((lists, width), BF16),
            pltpu.VMEM((owners, 8, 128), F32),
            pltpu.VMEM((owners, 8, 128), F32),
            pltpu.VMEM((8, places), I32),
            pltpu.VMEM((places, 128), I32),
            pltpu.VMEM((8, rows), I32),
            pltpu.VMEM((rows, 128), I32),
            pltpu.VMEM((lists, 128), F32),
            pltpu.VMEM((groups, 8, lists), F32),
            pltpu.VMEM((lists, 128), F32),
            dma((steps + 1,)),
            dma((steps + 1,)),
            dma,
            dma,
            dma((steps,)),
            dma((steps,)),
            dma((steps,)),
            dma((steps,)),
            dma,
            dma,
            dma((steps, groups)),
            dma((steps, groups)),
            dma,
            dma,
        ],
        compiler_params=pltpu.CompilerParams(
            collective_id=0, has_side_effects=True, vmem_limit_bytes=60 * 1024 * 1024
        ),
        cost_estimate=pl.CostEstimate(flops=30_000_000_000, bytes_accessed=14_000_000, transcendentals=0),
    )(vectors, owner_route[:, :, 0], list_slot, centroids, counts.reshape(1, lists))


def solution(mesh):
    in_specs = (
        P(None, ("grp", "list"), None),
        P(None, ("grp", "list"), None),
        P(None, ("grp", "list")),
        P("list", None),
        P("list"),
    )
    out_specs = (P(None, ("grp", "list"), None), P("list", None))
    return jax.shard_map(local, mesh=mesh, in_specs=in_specs, out_specs=out_specs, check_vma=False)
```

time: 463 us -> 238 us (0.51)
  waiting for transfers between devices: 278 us -> 0 us
  Pallas kernels: 0 us -> 230 us
  local copies, waits for them, and re-layouts: 63.3 us -> 7.33 us
  starting transfers between devices: 48.2 us -> 0 us
  other arithmetic: 31.4 us -> 0 us
  matrix products: 14.1 us -> 0 us
  between operations: 14.1 us -> 0.65 us
  blocking collectives: 10.8 us -> 0 us
    pallas_call x0 -> x1, Pallas kernels: none -> 230 us  [local(): pl.pallas_call(functools.partial(kernel, dims), out_shape=(jax.ShapeDtype...]
    psum x1 -> x0, waiting for transfers between devices: 191 us -> none  [local(): lax.psum(sums.astype(jnp.bfloat16), 'grp').astype(jnp.float32)]
    all_to_all x9 -> x0, waiting for transfers between devices: 87 us -> none  [the longest x3 56.9 us: local(): lax.all_to_all(send_rows, 'list', split_axis=0, concat_axis=0, tiled=True)]
    all_to_all x9 -> x0, starting transfers between devices: 48.2 us -> none  [the longest x3 18.1 us: route_fn(): lax.all_to_all(residual_rows, 'list', split_axis=0, concat_axis=0, tiled=...]
    gather x6 -> x0, local copies, waits for them, and re-layouts: 37 us -> none  [the longest x3 25.8 us: route_fn(): chosen = table[jnp.clip(list_ids, 0, list_dev - 1)]]
    scatter x6 -> x0, local copies, waits for them, and re-layouts: 23.4 us -> none  [the longest x3 14.4 us: local(): send_rows = jnp.zeros((owner_count * capacity, width), jnp.bfloat16).at[d...]
    convert_element_type x7 -> x0, other arithmetic: 14.9 us -> none  [the longest x3 14.9 us: route_fn(): residual_rows = (vec_rows.astype(jnp.float32) - chosen).astype(jnp.bfloat16)]
    dot_general x3 -> x0, matrix products: 14.1 us -> none  [list_sums(): sums = jnp.dot(one_hot, rows, preferred_element_type=jnp.float32)]
  transfers between devices with their start and end apart: 10 -> 0, of which waited for: 6 -> 0; matrix products, arithmetic and copies ran while one was open for 19% -> 0% of each run, Pallas kernels for 0% -> 0%
where the time goes in v1:
time: 238 us
  Pallas kernels  230 us (97%)
  local copies, waits for them, and re-layouts  7.33 us (3%)
    pallas_call x1, Pallas kernels, local(): pl.pallas_call(functools.partial(kernel, dims), out_shape=(jax.ShapeDtype...  230 us
    unnamed x5, local copies, waits for them, and re-layouts  7.33 us

profile of v1, /device:TPU:3, one launch (start us, length us, event | category | flops | bytes accessed | tf_op | source)
XLA Modules:
  0.0 238.0 jit_solution(13427169205926101338)
XLA Ops:
  0.6 1.3 copy.9
  1.9 230.0 %shard_map.68 = (bf16[3,512,1024]{2,1,0:T(8,128)(2,1)}, f32[1024,1024]{1,0:T(8,128)}) custom-call(bf16[3,512,1024]{2,1,0:T(8,128)(2,1)} %vec_hbm.1, s32[3,512]{1,0:T(4,128)} %bitcast.4, s32[3,512]{1,0:T(4,128)} %slot_ref.1, f32[1024,1024]{1,0:T(8,128)} %cent_hbm.1, s32[1,1024]{1,0:T(1,128)} %bitcast.5), custom_call_target="tpu_custom_call" | custom-call | flops 30000001024 | bytes 14000000 | tf_op jit(solution)/shard_map/pallas_call | solution.py:433
  231.9 0.0 copy-start
  232.0 4.0 %copy.12 = bf16[3,512,1024]{2,1,0:T(8,128)(2,1)} copy(bf16[3,512,1024]{2,1,0:T(8,128)(2,1)} %get-tuple-element.4) | data formatting | bytes 6291456
  236.0 0.0 copy-done
  236.0 2.0 copy.13
Async XLA Ops:
  231.9 4.0 %copy-start = (f32[1024,1024]{1,0:T(8,128)S(1)}, f32[1024,1024]{1,0:T(8,128)}, u32[]{:S(2)}) copy-start(f32[1024,1024]{1,0:T(8,128)} %get-tuple-element.5) | copy-start | bytes 12582916

commit v2 on v1

v2 whole, which is shorter than its diff:
```python
import functools

import jax
import jax.numpy as jnp
from jax import lax
from jax.experimental import pallas as pl
from jax.experimental.pallas import tpu as pltpu
from jax.sharding import PartitionSpec as P

MESH = pl.DeviceIdType.MESH
WIDE = 256
BF16 = jnp.bfloat16
F32 = jnp.float32
I32 = jnp.int32


def one_hot(mask):
    return jnp.where(mask, 1.0, 0.0).astype(BF16)


def dot(a, b):
    return jnp.dot(a, b, preferred_element_type=F32)


def loop(count, body):
    def step(i, carry):
        body(i)
        return carry

    lax.fori_loop(0, count, step, 0)


def cols(c):
    return pl.ds(c * WIDE, WIDE)


def rows_at(start, size):
    return pl.ds(pl.multiple_of(start, size), size)


def kernel(
    dims,
    vec_hbm, owner_ref, slot_ref, cent_hbm, counts_ref,
    out_hbm, new_hbm,
    vec, send, recv, back, part, from_left, from_right, num, high, low, pack_mat, unpack_mat, list_mat, pick_mat,
    send_slots, recv_slots, slot_row, slot_col, dest_row, dest_col, count_col, count_msg, weight_col,
    load_sem, out_sem, slot_send, slot_recv, disp_send, disp_recv, ret_send, ret_recv,
    right_send, left_send, left_recv, right_recv, cnt_send, cnt_recv,
):
    steps, rows, width, owners, groups, lists, cap = dims
    places = owners * cap
    half = lists // 2
    chunks = width // WIDE
    assert groups == 4
    pack = 128 // cap
    me = lax.axis_index("list")
    z = lax.axis_index("grp")

    loads = [pltpu.make_async_copy(vec_hbm.at[s], vec.at[s], load_sem.at[s]) for s in range(steps)]
    for c in range(chunks):
        loads.append(pltpu.make_async_copy(cent_hbm.at[:, cols(c)], num.at[c], load_sem.at[steps + c]))
    for load in loads:
        load.start()

    barrier = pltpu.get_barrier_semaphore()

    def greet_owner(i):
        pl.semaphore_signal(barrier, inc=1, device_id={"list": lax.rem(me + i + 1, owners)}, device_id_type=MESH)

    def greet_group(i):
        pl.semaphore_signal(barrier, inc=1, device_id={"grp": lax.rem(z + i + 1, groups)}, device_id_type=MESH)

    loop(owners - 1, greet_owner)
    loop(groups - 1, greet_group)

    owner_iota = lax.broadcasted_iota(I32, (owners, rows), 0)
    before = one_hot(
        lax.broadcasted_iota(I32, (rows, rows), 0) < lax.broadcasted_iota(I32, (rows, rows), 1)
    )
    hits, ranks, dests = [], [], []
    for s in range(steps):
        hit = jnp.where(owner_iota == owner_ref[s : s + 1, :], 1.0, 0.0)
        rank = hit * dot(hit.astype(BF16), before)
        hits.append(hit)
        ranks.append(jnp.sum(rank, axis=0, keepdims=True))
        dests.append(jnp.sum(rank + hit * (owner_iota * cap).astype(F32), axis=0, keepdims=True))
        dest_row[s : s + 1, :] = dests[s].astype(I32)
    table = jnp.concatenate(dests + ranks + [jnp.zeros((128 - 2 * steps, rows), F32)], axis=0)
    dest_col[...] = jnp.transpose(table).astype(I32)

    send_slots[...] = jnp.zeros_like(send_slots)
    lane = lax.broadcasted_iota(I32, (rows, 128), 1)
    for s in range(steps):
        value = slot_ref[s : s + 1, :] + 1
        upper = (value // 32).astype(F32)
        lower = (value % 32).astype(F32)
        spot = one_hot(lane == dest_col[:, steps + s : steps + s + 1] + lax.rem(me, pack) * cap)
        line = 32.0 * dot((hits[s] * upper).astype(BF16), spot) + dot((hits[s] * lower).astype(BF16), spot)
        for p in range(owners):
            send_slots[p, s : s + 1, :] = line[p : p + 1, :]
    recv_slots[me] = send_slots[me]

    pl.semaphore_wait(barrier, owners - 1 + groups - 1)

    def send_slot(i):
        p = lax.rem(me + i + 1, owners)
        pltpu.make_async_remote_copy(
            src_ref=send_slots.at[p], dst_ref=recv_slots.at[me], send_sem=slot_send, recv_sem=slot_recv,
            device_id={"list": p}, device_id_type=MESH,
        ).start()

    loop(owners - 1, send_slot)

    tile = min(256, places)
    list_tile = min(256, half)
    row_tile = min(256, rows)

    def pack_rows(s, c):
        if c == 0:
            loads[s].wait()
            place = lax.broadcasted_iota(I32, (places, rows), 0)
            pack_mat[...] = one_hot(place == dest_row[s : s + 1, :])

        def body(i):
            at = rows_at(i * tile, tile)
            send[s, c, at, :] = dot(pack_mat[at, :], vec[s, :, cols(c)]).astype(BF16)

        loop(places // tile, body)
        mine = rows_at(me * cap, cap)
        recv[s, c, mine, :] = send[s, c, mine, :]

    def exchange(src, dst, s, c, send_sem, recv_sem):
        def body(i):
            p = lax.rem(me + i + 1, owners)
            pltpu.make_async_remote_copy(
                src_ref=src.at[s, c, rows_at(p * cap, cap)], dst_ref=dst.at[s, c, rows_at(me * cap, cap)],
                send_sem=send_sem.at[s, c], recv_sem=recv_sem.at[s, c],
                device_id={"list": p}, device_id_type=MESH,
            ).start()

        loop(owners - 1, body)

    def dispatch(s, c):
        exchange(send, recv, s, c, disp_send, disp_recv)

    def drain(ref, s, c, sem):
        others = ref.at[s, c, pl.ds(0, (owners - 1) * cap)]
        pltpu.make_async_copy(others, others, sem.at[s, c]).wait()

    def split_table():
        for c in range(chunks):
            loads[steps + c].wait()

        def body(c):
            value = num[c]
            top = value.astype(BF16)
            high[c] = top
            low[c] = (value - top.astype(F32)).astype(BF16)

        loop(chunks, body)

    def get_slots():
        others = recv_slots.at[pl.ds(0, owners - 1)]
        pltpu.make_async_copy(others, others, slot_recv).wait()
        pieces = []
        for c in range(owners // pack):
            piece = recv_slots[c * pack]
            for i in range(1, pack):
                piece = piece + recv_slots[c * pack + i]
            pieces.append(piece)
        line = jnp.concatenate(pieces, axis=1) - 1.0
        slot_row[...] = line.astype(I32)
        tall = jnp.concatenate([line, jnp.zeros((120, places), F32)], axis=0)
        slot_col[...] = jnp.transpose(tall).astype(I32)

    def send_counts():
        count_col[...] = jnp.zeros_like(count_col)

        def body(i):
            at = rows_at(i * list_tile, list_tile)
            name = lax.broadcasted_iota(I32, (list_tile, places), 0) + i * list_tile
            column = lax.broadcasted_iota(I32, (list_tile, 128), 1)
            for s in range(steps):
                found = jnp.sum(jnp.where(name == slot_row[s : s + 1, :], 1.0, 0.0), axis=1, keepdims=True)
                count_col[at, :] = jnp.where(column == s, found, count_col[at, :])

        loop(lists // list_tile, body)
        count_msg[z] = jnp.transpose(count_col[...])[0:8, :]

        def share(i):
            g = lax.rem(z + i + 1, groups)
            pltpu.make_async_remote_copy(
                src_ref=count_msg.at[z], dst_ref=count_msg.at[z], send_sem=cnt_send, recv_sem=cnt_recv,
                device_id={"grp": g}, device_id_type=MESH,
            ).start()

        loop(groups - 1, share)

    def get_counts():
        others = count_msg.at[pl.ds(0, groups - 1)]
        pltpu.make_async_copy(others, others, cnt_recv).wait()
        total = count_msg[0]
        for g in range(1, groups):
            total = total + count_msg[g]
        lines = [counts_ref[...].astype(F32)]
        for s in range(steps):
            lines.append(lines[-1] + total[s : s + 1, :])
        lines.append(jnp.ones((128 - len(lines), lists), F32))
        weight_col[...] = jnp.transpose(jnp.concatenate(lines, axis=0))

    def list_sums(s, c):
        if c == 0:
            name = lax.broadcasted_iota(I32, (lists, places), 0)
            list_mat[...] = one_hot(name == slot_row[s : s + 1, :])
        first = (s * chunks + c) * 2
        for h in range(2):
            def body(i):
                at = rows_at(h * half + i * list_tile, list_tile)
                value = dot(list_mat[at, :], recv[s, c]).astype(BF16)
                to = rows_at(i * list_tile, list_tile)
                part[first, h, to, :] = value[:, :128]
                part[first + 1, h, to, :] = value[:, 128:]

            loop(half // list_tile, body)

    def residual(s, c):
        if c == 0:
            name = lax.broadcasted_iota(I32, (places, lists), 1)
            pick_mat[...] = one_hot(name == slot_col[:, s : s + 1])

        def body(i):
            at = rows_at(i * tile, tile)
            chosen = dot(pick_mat[at, :], high[c]) + dot(pick_mat[at, :], low[c])
            recv[s, c, at, :] = (recv[s, c, at, :].astype(F32) - chosen).astype(BF16)

        loop(places // tile, body)
        mine = rows_at(me * cap, cap)
        back[s, c, mine, :] = recv[s, c, mine, :]
        exchange(recv, back, s, c, ret_send, ret_recv)

    def out_copy(s, c):
        return pltpu.make_async_copy(vec.at[s, :, cols(c)], out_hbm.at[s, :, cols(c)], out_sem.at[s, c])

    def unpack_rows(s, c):
        if c == 0:
            name = lax.broadcasted_iota(I32, (rows, places), 1)
            unpack_mat[...] = one_hot(name == dest_col[:, s : s + 1])
        drain(back, s, c, ret_recv)

        def body(i):
            at = rows_at(i * row_tile, row_tile)
            vec[s, at, cols(c)] = dot(unpack_mat[at, :], back[s, c]).astype(BF16)

        loop(rows // row_tile, body)
        out_copy(s, c).start()

    def new_copy(c):
        return pltpu.make_async_copy(num.at[c], new_hbm.at[:, cols(c)], out_sem.at[steps, c])

    def wait_left(j, h):
        pltpu.make_async_copy(from_left.at[j, h], from_left.at[j, h], left_recv.at[j, h]).wait()

    def wait_right(j, h):
        pltpu.make_async_copy(from_right.at[j, h], from_right.at[j, h], right_recv.at[j, h]).wait()

    def to_right(src, j, h):
        pltpu.make_async_remote_copy(
            src_ref=src.at[j, h], dst_ref=from_left.at[j, h], send_sem=right_send, recv_sem=left_recv.at[j, h],
            device_id={"grp": lax.rem(z + 1, groups)}, device_id_type=MESH,
        ).start()

    def to_left(src, j, h):
        pltpu.make_async_remote_copy(
            src_ref=src.at[j, h], dst_ref=from_right.at[j, h], send_sem=left_send, recv_sem=right_recv.at[j, h],
            device_id={"grp": lax.rem(z + groups - 1, groups)}, device_id_type=MESH,
        ).start()

    def update(s, c):
        first = (s * chunks + c) * 2
        last = s == steps - 1

        @pl.when(z == 0)
        def _():
            for i in range(2):
                wait_right(first + i, 0)
                wait_right(first + i, 1)

        @pl.when(z == groups - 1)
        def _():
            for i in range(2):
                wait_left(first + i, 0)
                wait_left(first + i, 1)

        def add(h, ref):
            def body(i):
                at = rows_at(h * half + i * list_tile, list_tile)
                of = rows_at(i * list_tile, list_tile)
                over = 1.0 / weight_col[at, s + 1 : s + 2]
                sums = jnp.concatenate([ref[first, h, of, :], ref[first + 1, h, of, :]], axis=1)
                value = num[c, at, :]
                if s == 0:
                    value = value * weight_col[at, 0:1]
                value = value + sums.astype(F32)
                mean = value * over
                if last:
                    num[c, at, :] = mean
                else:
                    num[c, at, :] = value
                    top = mean.astype(BF16)
                    high[c, at, :] = top
                    low[c, at, :] = (mean - top.astype(F32)).astype(BF16)

            loop(half // list_tile, body)

        for h in range(2):
            pl.when(z < 1 + h)(functools.partial(add, h, from_right))
            pl.when(z == 1 + h)(functools.partial(add, h, part))
            pl.when(z > 1 + h)(functools.partial(add, h, from_left))
        if last:
            new_copy(c).start()

    pairs = 2 * steps * chunks

    def relay(t):
        def at_lag(lag, who, body):
            @pl.when((z == who) & (t - lag >= 0) & (t - lag < pairs))
            def _():
                body(t - lag)

        def left_end(j):
            to_right(part, j, 1)
            to_right(part, j, 0)

        def right_end(j):
            to_left(part, j, 0)
            to_left(part, j, 1)

        def pass_right(j):
            wait_left(j, 1)
            from_left[j, 1] = (from_left[j, 1].astype(F32) + part[j, 1].astype(F32)).astype(BF16)
            to_right(from_left, j, 1)

        def pass_left(j):
            wait_right(j, 0)
            from_right[j, 0] = (from_right[j, 0].astype(F32) + part[j, 0].astype(F32)).astype(BF16)
            to_left(from_right, j, 0)

        def total(h, j):
            wait_left(j, h)
            wait_right(j, h)
            value = part[j, h].astype(F32) + from_left[j, h].astype(F32) + from_right[j, h].astype(F32)
            part[j, h] = value.astype(BF16)
            to_right(part, j, h)
            to_left(part, j, h)

        def forward_left(j):
            wait_right(j, 1)
            to_left(from_right, j, 1)

        def forward_right(j):
            wait_left(j, 0)
            to_right(from_left, j, 0)

        at_lag(0, 0, left_end)
        at_lag(0, 3, right_end)
        at_lag(1, 1, pass_right)
        at_lag(1, 2, pass_left)
        at_lag(2, 1, functools.partial(total, 0))
        at_lag(2, 2, functools.partial(total, 1))
        at_lag(3, 1, forward_left)
        at_lag(3, 2, forward_right)

    ready, after = {}, {}

    def plan(table, turn, *tasks):
        table.setdefault(turn, []).extend(tasks)

    call = functools.partial
    for c in range(chunks):
        if c + 2 < chunks:
            plan(ready, c, call(drain, recv, 0, c, disp_recv), call(dispatch, 0, c + 2))
        else:
            plan(ready, c, call(drain, recv, 0, c, disp_recv))
        plan(ready, c, call(list_sums, 0, c))
        for s in range(1, steps):
            plan(ready, s * chunks + c, call(drain, recv, s, c, disp_recv), call(list_sums, s, c))
    plan(after, 0, *[call(pack_rows, 1, c) for c in range(chunks)], send_counts, split_table)
    plan(after, 3, get_counts)
    for c in range(chunks):
        plan(after, c, call(residual, 0, c))
        if c == chunks - 2:
            for d in range(chunks):
                plan(after, c, call(dispatch, 1, d))
        if c == chunks - 1:
            plan(after, c, *[call(pack_rows, 2, d) for d in range(chunks)])
    for c in range(chunks):
        plan(after, chunks + c, call(dispatch, 2, c))
    for s in range(steps):
        for c in range(chunks):
            plan(after, s * chunks + c + 3, call(update, s, c))
            if s + 1 < steps:
                plan(after, max((s + 1) * chunks + c, s * chunks + c + 3), call(residual, s + 1, c))
                plan(after, (s + 1) * chunks + c + 1, call(unpack_rows, s, c))

    pack_rows(0, 0)
    dispatch(0, 0)
    pack_rows(0, 1)
    dispatch(0, 1)
    for c in range(2, chunks):
        pack_rows(0, c)
    get_slots()

    for turn in range(steps * chunks + 3):
        for task in ready.get(turn, []):
            task()
        if turn < steps * chunks + 2:
            relay(2 * turn)
            relay(2 * turn + 1)
        for task in after.get(turn, []):
            task()
    for c in range(chunks):
        unpack_rows(steps - 1, c)

    others = send_slots.at[pl.ds(0, owners - 1)]
    pltpu.make_async_copy(others, others, slot_send).wait()
    others = count_msg.at[pl.ds(0, groups - 1)]
    pltpu.make_async_copy(others, others, cnt_send).wait()
    for s in range(steps):
        for c in range(chunks):
            drain(send, s, c, disp_send)
            drain(recv, s, c, ret_send)
            out_copy(s, c).wait()

    @pl.when(z < groups - 1)
    def _():
        pltpu.make_async_copy(from_left, from_left, right_send).wait()

    @pl.when(z > 0)
    def _():
        pltpu.make_async_copy(from_right, from_right, left_send).wait()

    for c in range(chunks):
        new_copy(c).wait()


def local(vectors, owner_route, list_slot, centroids, counts):
    steps, rows, width = vectors.shape
    owners = lax.axis_size("list")
    groups = lax.axis_size("grp")
    lists = centroids.shape[0]
    cap = 2 * rows // owners
    places = owners * cap
    half = lists // 2
    chunks = width // WIDE
    pairs = 2 * steps * chunks
    dims = (steps, rows, width, owners, groups, lists, cap)
    vmem = pl.BlockSpec(memory_space=pltpu.VMEM)
    hbm = pl.BlockSpec(memory_space=pl.ANY)
    dma = pltpu.SemaphoreType.DMA
    return pl.pallas_call(
        functools.partial(kernel, dims),
        out_shape=(
            jax.ShapeDtypeStruct((steps, rows, width), BF16),
            jax.ShapeDtypeStruct((lists, width), F32),
        ),
        in_specs=[hbm, vmem, vmem, hbm, vmem],
        out_specs=(hbm, hbm),
        scratch_shapes=[
            pltpu.VMEM((steps, rows, width), BF16),
            pltpu.VMEM((steps, chunks, places, WIDE), BF16),
            pltpu.VMEM((steps, chunks, places, WIDE), BF16),
            pltpu.VMEM((steps, chunks, places, WIDE), BF16),
            pltpu.VMEM((pairs, 2, half, 128), BF16),
            pltpu.VMEM((pairs, 2, half, 128), BF16),
            pltpu.VMEM((pairs, 2, half, 128), BF16),
            pltpu.VMEM((chunks, lists, WIDE), F32),
            pltpu.VMEM((chunks, lists, WIDE), BF16),
            pltpu.VMEM((chunks, lists, WIDE), BF16),
            pltpu.VMEM((places, rows), BF16),
            pltpu.VMEM((rows, places), BF16),
            pltpu.VMEM((lists, places), BF16),
            pltpu.VMEM((places, lists), BF16),
            pltpu.VMEM((owners, 8, 128), F32),
            pltpu.VMEM((owners, 8, 128), F32),
            pltpu.VMEM((8, places), I32),
            pltpu.VMEM((places, 128), I32),
            pltpu.VMEM((8, rows), I32),
            pltpu.VMEM((rows, 128), I32),
            pltpu.VMEM((lists, 128), F32),
            pltpu.VMEM((groups, 8, lists), F32),
            pltpu.VMEM((lists, 128), F32),
            dma((steps + chunks,)),
            dma((steps + 1, chunks)),
            dma,
            dma,
            dma((steps, chunks)),
            dma((steps, chunks)),
            dma((steps, chunks)),
            dma((steps, chunks)),
            dma,
            dma,
            dma((pairs, 2)),
            dma((pairs, 2)),
            dma,
            dma,
        ],
        compiler_params=pltpu.CompilerParams(
            collective_id=0, has_side_effects=True, vmem_limit_bytes=62 * 1024 * 1024
        ),
        cost_estimate=pl.CostEstimate(flops=30_000_000_000, bytes_accessed=14_000_000, transcendentals=0),
    )(vectors, owner_route[:, :, 0], list_slot, centroids, counts.reshape(1, lists))


def solution(mesh):
    in_specs = (
        P(None, ("grp", "list"), None),
        P(None, ("grp", "list"), None),
        P(None, ("grp", "list")),
        P("list", None),
        P("list"),
    )
    out_specs = (P(None, ("grp", "list"), None), P("list", None))
    return jax.shard_map(local, mesh=mesh, in_specs=in_specs, out_specs=out_specs, check_vma=False)
```

time: 238 us -> 192 us (0.81); the launches traced: 238 us -> 189 us
  Pallas kernels: 230 us -> 181 us
    pallas_call x1, Pallas kernels: 230 us -> 181 us  [local(): pl.pallas_call(functools.partial(kernel, dims), out_shape=(jax.ShapeDtype...]
where the time goes in v2:
time: 192 us; the launch traced here: 189 us
  Pallas kernels  181 us (94%)
  local copies, waits for them, and re-layouts  7.33 us (4%)
    pallas_call x1, Pallas kernels, local(): pl.pallas_call(functools.partial(kernel, dims), out_shape=(jax.ShapeDtype...  181 us
    unnamed x5, local copies, waits for them, and re-layouts  7.33 us

profile of v2, /device:TPU:3, one launch (start us, length us, event | category | flops | bytes accessed | tf_op | source)
XLA Modules:
  0.0 188.9 jit_solution(13632824399580452083)
XLA Ops:
  0.6 1.3 copy.9
  1.9 180.9 %shard_map.68 = (bf16[3,512,1024]{2,1,0:T(8,128)(2,1)}, f32[1024,1024]{1,0:T(8,128)}) custom-call(bf16[3,512,1024]{2,1,0:T(8,128)(2,1)} %vec_hbm.1, s32[3,512]{1,0:T(4,128)} %bitcast.4, s32[3,512]{1,0:T(4,128)} %slot_ref.1, f32[1024,1024]{1,0:T(8,128)} %cent_hbm.1, s32[1,1024]{1,0:T(1,128)} %bitcast.5), custom_call_target="tpu_custom_call" | custom-call | flops 30000001024 | bytes 14000000 | tf_op jit(solution)/shard_map/pallas_call | solution.py:460
  182.8 0.0 copy-start
  182.8 4.0 %copy.12 = bf16[3,512,1024]{2,1,0:T(8,128)(2,1)} copy(bf16[3,512,1024]{2,1,0:T(8,128)(2,1)} %get-tuple-element.4) | data formatting | bytes 6291456
  186.9 0.0 copy-done
  186.9 2.0 %copy.13 = f32[1024,1024]{1,0:T(8,128)} copy(f32[1024,1024]{1,0:T(8,128)S(1)} %copy-done) | data formatting | bytes 8388608
Async XLA Ops:
  182.8 4.0 %copy-start = (f32[1024,1024]{1,0:T(8,128)S(1)}, f32[1024,1024]{1,0:T(8,128)}, u32[]{:S(2)}) copy-start(f32[1024,1024]{1,0:T(8,128)} %get-tuple-element.5) | copy-start | bytes 12582916

commit v3 on v2

--- a/solution.py
+++ b/solution.py
@@ -147,17 +147,17 @@
         others = ref.at[s, c, pl.ds(0, (owners - 1) * cap)]
         pltpu.make_async_copy(others, others, sem.at[s, c]).wait()
 
-    def split_table():
-        for c in range(chunks):
-            loads[steps + c].wait()
-
-        def body(c):
-            value = num[c]
+    def split_table(c):
+        loads[steps + c].wait()
+
+        def body(i):
+            at = rows_at(i * list_tile, list_tile)
+            value = num[c, at, :]
             top = value.astype(BF16)
-            high[c] = top
-            low[c] = (value - top.astype(F32)).astype(BF16)
-
-        loop(chunks, body)
+            high[c, at, :] = top
+            low[c, at, :] = (value - top.astype(F32)).astype(BF16)
+
+        loop(lists // list_tile, body)
 
     def get_slots():
         others = recv_slots.at[pl.ds(0, owners - 1)]
@@ -384,23 +384,19 @@
         plan(ready, c, call(list_sums, 0, c))
         for s in range(1, steps):
             plan(ready, s * chunks + c, call(drain, recv, s, c, disp_recv), call(list_sums, s, c))
-    plan(after, 0, *[call(pack_rows, 1, c) for c in range(chunks)], send_counts, split_table)
+    plan(after, 1, send_counts)
     plan(after, 3, get_counts)
     for c in range(chunks):
-        plan(after, c, call(residual, 0, c))
-        if c == chunks - 2:
-            for d in range(chunks):
-                plan(after, c, call(dispatch, 1, d))
-        if c == chunks - 1:
-            plan(after, c, *[call(pack_rows, 2, d) for d in range(chunks)])
-    for c in range(chunks):
-        plan(after, chunks + c, call(dispatch, 2, c))
+        turn = min(max(c, 1), chunks - 1)
+        plan(after, turn, call(pack_rows, 1, c), call(dispatch, 1, c))
+        plan(after, c + 1, call(split_table, c), call(residual, 0, c))
+        plan(after, chunks + c, call(pack_rows, 2, c), call(dispatch, 2, c))
     for s in range(steps):
         for c in range(chunks):
             plan(after, s * chunks + c + 3, call(update, s, c))
             if s + 1 < steps:
                 plan(after, max((s + 1) * chunks + c, s * chunks + c + 3), call(residual, s + 1, c))
-                plan(after, (s + 1) * chunks + c + 1, call(unpack_rows, s, c))
+            plan(after, min(s * chunks + c + 3, steps * chunks + 1), call(unpack_rows, s, c))
 
     pack_rows(0, 0)
     dispatch(0, 0)
@@ -413,13 +409,17 @@
     for turn in range(steps * chunks + 3):
         for task in ready.get(turn, []):
             task()
-        if turn < steps * chunks + 2:
+        tasks = after.get(turn, [])
+        middle = len(tasks) // 2
+        relays = turn < steps * chunks + 2
+        if relays:
             relay(2 * turn)
+        for task in tasks[:middle]:
+            task()
+        if relays:
             relay(2 * turn + 1)
-        for task in after.get(turn, []):
+        for task in tasks[middle:]:
             task()
-    for c in range(chunks):
-        unpack_rows(steps - 1, c)
 
     others = send_slots.at[pl.ds(0, owners - 1)]
     pltpu.make_async_copy(others, others, slot_send).wait()

time: 192 us -> 185 us (0.964); the launches traced: 189 us -> 184 us
  Pallas kernels: 181 us -> 176 us
    pallas_call x1, Pallas kernels: 181 us -> 176 us  [local(): pl.pallas_call(functools.partial(kernel, dims), out_shape=(jax.ShapeDtype...]
where the time goes in v3:
time: 185 us; the launch traced here: 184 us
  Pallas kernels  176 us (95%)
  local copies, waits for them, and re-layouts  7.33 us (4%)
    pallas_call x1, Pallas kernels, local(): pl.pallas_call(functools.partial(kernel, dims), out_shape=(jax.ShapeDtype...  176 us
    unnamed x5, local copies, waits for them, and re-layouts  7.33 us

profile of v3, /device:TPU:3, one launch (start us, length us, event | category | flops | bytes accessed | tf_op | source)
XLA Modules:
  0.0 184.4 jit_solution(14145007345948676482)
XLA Ops:
  0.6 1.3 copy.9
  1.9 176.4 %shard_map.68 = (bf16[3,512,1024]{2,1,0:T(8,128)(2,1)}, f32[1024,1024]{1,0:T(8,128)}) custom-call(bf16[3,512,1024]{2,1,0:T(8,128)(2,1)} %vec_hbm.1, s32[3,512]{1,0:T(4,128)} %bitcast.4, s32[3,512]{1,0:T(4,128)} %slot_ref.1, f32[1024,1024]{1,0:T(8,128)} %cent_hbm.1, s32[1,1024]{1,0:T(1,128)} %bitcast.5), custom_call_target="tpu_custom_call" | custom-call | flops 30000001024 | bytes 14000000 | tf_op jit(solution)/shard_map/pallas_call | solution.py:460
  178.3 0.0 copy-start
  178.3 4.0 %copy.12 = bf16[3,512,1024]{2,1,0:T(8,128)(2,1)} copy(bf16[3,512,1024]{2,1,0:T(8,128)(2,1)} %get-tuple-element.4) | data formatting | bytes 6291456
  182.4 0.0 copy-done
  182.4 2.0 %copy.13 = f32[1024,1024]{1,0:T(8,128)} copy(f32[1024,1024]{1,0:T(8,128)S(1)} %copy-done) | data formatting | bytes 8388608
Async XLA Ops:
  178.3 4.0 %copy-start = (f32[1024,1024]{1,0:T(8,128)S(1)}, f32[1024,1024]{1,0:T(8,128)}, u32[]{:S(2)}) copy-start(f32[1024,1024]{1,0:T(8,128)} %get-tuple-element.5) | copy-start | bytes 12582916
